TPU v7x, 32 devices: a whole 2x2x4 slice. The times are simulated.
32 devices in a mesh: dp: 4 (over y, x), pipe: 4 (over z), tensor: 2 (over core).
Axes of the slice: x: 2, y: 2, z: 4, core: 2. Of those that a mesh axis runs over, the one named last changes fastest.
Arguments:
- tokens: bfloat16 [2048, 3072], P(('dp', 'tensor')), may hold values from -6 to 6
- destination: int32 [2048], P(('dp', 'tensor')), may hold values from 0 to 2047, as said below
- segments: int32 [16, 128], P('dp'), may hold values from 0 to 5, never falling along the last dimension, each value on 1 to 64 neighbouring positions
- query_weight: bfloat16 [4, 3072, 2048], P('pipe', None, 'tensor')
- key_value_weight: bfloat16 [4, 3072, 2048], P('pipe', None, 'tensor')
- out_weight: bfloat16 [4, 2048, 3072], P('pipe', 'tensor'), may hold values from -0.125 to 0.125
- gate_weight: bfloat16 [4, 3072, 8192], P('pipe', None, 'tensor'), may hold values from -0.109375 to 0.109375
- up_weight: bfloat16 [4, 3072, 8192], P('pipe', None, 'tensor'), may hold values from -0.109375 to 0.109375
- down_weight: bfloat16 [4, 8192, 3072], P('pipe', 'tensor'), may hold values from -0.0625 to 0.0625
- attention_gain: float32 [4, 3072], P('pipe'), may hold values from 0.1 to 1.9
- forward_gain: float32 [4, 3072], P('pipe'), may hold values from 0.1 to 1.9
Outputs:
- layers_out: float32 [2048, 3072], P(('dp', 'pipe', 'tensor'))
Inputs may be any that keep to these rules, and one draw needn't show every extreme that they name: destination is a permutation of the 2048 rows. A row held at tensor index t goes to a place within its micro-batch in [t * 64, (t + 1) * 64). At most 128 rows of one device go to one dp index, and every device sends exactly 128 rows to some dp index.
All inputs are finite; a program needn't handle non-finite values.
Results may differ from a plain program's by a relative error of at most 0.04.
Values may be sent and summed in bfloat16 or wider, within the bound.
A program may use at most 192 MiB of HBM per device.

v0:
```python
import jax
import jax.numpy as jnp
from jax import lax
from jax.sharding import PartitionSpec as P

KV = 8
HD = 128


def swapped(value, axis, apart):
    mask = 2**apart
    pairs = [(source, source ^ mask) for source in range(lax.axis_size(axis))]
    return lax.ppermute(value, axis, pairs)


def shifted(array, axis, by):
    peers = lax.axis_size(axis)
    pairs = [(i, i + by) for i in range(peers) if 0 <= i + by < peers]
    return lax.ppermute(array, axis, pairs)


def broadcast(block, axis, source):
    block = jnp.where(lax.axis_index(axis) == source, block, jnp.zeros_like(block))
    return lax.psum(block, axis)


def doc_positions(doc_ids):
    order = jnp.arange(doc_ids.shape[0], dtype=jnp.int32)
    change = jnp.concatenate([jnp.ones((1,), dtype=bool), doc_ids[1:] != doc_ids[:-1]])
    starts = lax.cummax(jnp.where(change, order, jnp.zeros_like(order)), axis=0)
    return (order - starts).astype(jnp.float32)


def rotate(stack, places):
    half_width = stack.shape[-1] // 2
    frequency = 500000.0 ** (-(jnp.arange(half_width, dtype=jnp.float32) * 2.0 / stack.shape[-1]))
    angles = places[:, None] * frequency[None, :]
    cosine = jnp.cos(angles)[:, None, :]
    sine_part = jnp.sin(angles)[:, None, :]
    front_half = stack[..., :half_width]
    back_half = stack[..., half_width:]
    return jnp.concatenate(
        [front_half * cosine - back_half * sine_part, back_half * cosine + front_half * sine_part],
        axis=-1,
    )


def normalize(rows_in, gain):
    meansq = jnp.mean(rows_in * rows_in, axis=-1, keepdims=True)
    return (rows_in * lax.rsqrt(meansq + 1e-05) * gain).astype(jnp.bfloat16)


def visible(doc_ids):
    order = jnp.arange(doc_ids.shape[0], dtype=jnp.int32)
    return jnp.logical_and(doc_ids[:, None] == doc_ids[None, :], order[None, :] <= order[:, None])


def attend(queries, key_heads, value_heads, doc_ids):
    rows, heads_here, head_width = queries.shape
    shared_heads = key_heads.shape[1]
    grouped_queries = queries.reshape(rows, shared_heads, heads_here // shared_heads, head_width)
    scores = jnp.einsum(
        "qagd,kad->agqk",
        grouped_queries,
        key_heads,
        precision=lax.Precision.HIGHEST,
        preferred_element_type=jnp.float32,
    ) * head_width ** (-0.5)
    scores = jnp.where(visible(doc_ids), scores, jnp.float32(-1e30))
    row_max = jnp.max(scores, axis=-1, keepdims=True)
    spread = jnp.exp(scores - row_max)
    weights = (spread / jnp.sum(spread, axis=-1, keepdims=True)).astype(jnp.bfloat16)
    mixed = jnp.einsum("agqk,kad->qagd", weights, value_heads, preferred_element_type=jnp.float32)
    return mixed.astype(jnp.bfloat16).reshape(rows, heads_here * head_width)


def expand(rows_in, gate_local, up_local):
    gate = jnp.dot(rows_in, gate_local, preferred_element_type=jnp.float32)
    upward = jnp.dot(rows_in, up_local, preferred_element_type=jnp.float32)
    return (jax.nn.silu(gate) * upward).astype(jnp.bfloat16)


def split_pairs(pairs, places, tensor_count):
    rows = pairs.shape[0]
    if tensor_count > KV:
        parity = lax.axis_index("tensor") % 2
        turned = rotate(pairs.reshape(rows, 1, HD), places).reshape(rows, HD)
        mine = jnp.where(parity == 0, turned, pairs)
        partner = swapped(mine.astype(jnp.bfloat16), "tensor", 0).astype(mine.dtype)
        key_heads = jnp.where(parity == 0, mine, partner).reshape(rows, 1, HD)
        value_heads = (
            jnp.where(parity == 0, partner, mine).astype(jnp.bfloat16).reshape(rows, 1, HD)
        )
    else:
        grouped = pairs.reshape(rows, -1, 2, HD)
        key_heads = rotate(grouped[:, :, 0], places)
        value_heads = grouped[:, :, 1].astype(jnp.bfloat16)
    return (key_heads, value_heads)


def run_layer(current, doc_ids, layer_weights):
    (
        query_local,
        pair_local,
        out_local,
        gate_local,
        up_local,
        down_local,
        gain_attention,
        gain_forward,
    ) = layer_weights
    tensor_count = lax.axis_size("tensor")
    micro_rows = doc_ids.shape[0]
    query_cols = query_local.shape[1]
    places = doc_positions(doc_ids)
    piece = lax.all_gather(normalize(current, gain_attention), "tensor", axis=0, tiled=True)
    projected = jnp.concatenate(
        [
            jnp.dot(piece, query_local, preferred_element_type=jnp.float32),
            jnp.dot(piece, pair_local, preferred_element_type=jnp.float32),
        ],
        axis=1,
    )
    heads_here = query_cols // HD
    queries = rotate(projected[:, :query_cols].reshape(micro_rows, heads_here, HD), places)
    key_heads, value_heads = split_pairs(projected[:, query_cols:], places, tensor_count)
    mixed = attend(queries, key_heads, value_heads, doc_ids)
    total = lax.psum_scatter(
        jnp.dot(mixed, out_local, preferred_element_type=jnp.float32).astype(jnp.bfloat16),
        "tensor",
        scatter_dimension=0,
        tiled=True,
    ).astype(jnp.float32)
    halfway = current + total
    hidden = expand(
        lax.all_gather(normalize(halfway, gain_forward), "tensor", axis=0, tiled=True),
        gate_local,
        up_local,
    )
    forward = lax.psum_scatter(
        jnp.dot(hidden, down_local, preferred_element_type=jnp.float32).astype(jnp.bfloat16),
        "tensor",
        scatter_dimension=0,
        tiled=True,
    ).astype(jnp.float32)
    return halfway + forward


def pass_on(result):
    return shifted(result.astype(jnp.bfloat16), "pipe", 1).astype(result.dtype)


def shards(
    tokens,
    destination,
    segments,
    query_weight,
    key_value_weight,
    out_weight,
    gate_weight,
    up_weight,
    down_weight,
    attention_gain,
    forward_gain,
):
    group_count = lax.axis_size("dp")
    tensor_count = lax.axis_size("tensor")
    pipe_count = lax.axis_size("pipe")
    micro_count, micro_rows = segments.shape
    slab_rows = micro_rows // tensor_count
    held_rows, width = tokens.shape
    capacity = held_rows // 2
    group_span = micro_count * micro_rows
    target = destination // group_span
    within = destination % group_span
    landing = within // micro_rows * slab_rows + within % slab_rows
    member = (target[:, None] == jnp.arange(group_count, dtype=jnp.int32)[None, :]).astype(
        jnp.int32
    )
    before = jnp.sum((jnp.cumsum(member, axis=0) - member) * member, axis=1)
    slot_index = target * capacity + before
    send_rows = jnp.zeros((group_count * capacity, width), jnp.bfloat16).at[slot_index].set(tokens)
    send_places = (
        jnp.full((group_count * capacity,), held_rows, jnp.int32).at[slot_index].set(landing)
    )
    got_rows, got_places = (
        lax.all_to_all(
            send_rows.reshape(group_count, capacity, width),
            "dp",
            split_axis=0,
            concat_axis=0,
            tiled=True,
        ),
        lax.all_to_all(
            send_places.reshape(group_count, capacity),
            "dp",
            split_axis=0,
            concat_axis=0,
            tiled=True,
        ),
    )
    regrouped = (
        jnp.zeros((held_rows, width), jnp.bfloat16)
        .at[got_places.reshape(-1)]
        .set(got_rows.reshape(-1, width), mode="drop")
    )
    micro_batches = regrouped.reshape(micro_count, slab_rows, width)
    layer_weights = (
        query_weight[0],
        key_value_weight[0],
        out_weight[0],
        gate_weight[0],
        up_weight[0],
        down_weight[0],
        attention_gain[0],
        forward_gain[0],
    )
    phase_index = lax.axis_index("pipe")
    carried = jnp.zeros((slab_rows, width), jnp.float32)
    finished = []
    for moment in range(micro_count + pipe_count - 1):
        feed_rows = micro_batches[min(moment, micro_count - 1)].astype(jnp.float32)
        current = jnp.where(
            jnp.logical_and(phase_index == 0, moment < micro_count), feed_rows, carried
        )
        micro_index = jnp.clip(moment - phase_index, 0, micro_count - 1)
        doc_ids = lax.dynamic_index_in_dim(segments, micro_index, 0, keepdims=False)
        result = run_layer(current, doc_ids, layer_weights)
        if moment >= pipe_count - 1:
            finished.append(result)
        if moment < micro_count + pipe_count - 2:
            carried = pass_on(result)
    everyone = broadcast(jnp.stack(finished).astype(jnp.bfloat16), "pipe", pipe_count - 1).astype(
        jnp.float32
    )
    return lax.dynamic_index_in_dim(everyone, phase_index, 0, keepdims=False)


def solution(mesh):
    placed = (
        P(("dp", "tensor"), None),
        P(("dp", "tensor")),
        P("dp", None),
        P("pipe", None, "tensor"),
        P("pipe", None, "tensor"),
        P("pipe", "tensor", None),
        P("pipe", None, "tensor"),
        P("pipe", None, "tensor"),
        P("pipe", "tensor", None),
        P("pipe", None),
        P("pipe", None),
    )
    return jax.shard_map(
        shards,
        mesh=mesh,
        in_specs=placed,
        out_specs=P(("dp", "pipe", "tensor"), None),
        check_vma=False,
    )
```

profile of v0, /device:TPU:16, one launch (start us, length us, event | category | flops | bytes accessed | tf_op | source)
XLA Modules:
  0.0 779.1 jit_solution(8876273520827627414)
XLA Ops:
  48.5 33.7 %all-to-all-done.1 = bf16[4,128,3072]{2,1,0:T(8,128)(2,1)S(1)} async-done(((bf16[4,128,3072]{2,1,0:T(8,128)(2,1)}), bf16[4,128,3072]{2,1,0:T(8,128)(2,1)S(1)}, u32[]{:S(2)}, u32[]{:S(2)}) %all-to-all-start.1) | async-done | bytes 3145760 | tf_op jit(solution)/shard_map/all_to_all | solution.py:187
  122.5 12.9 %fusion.47 = f32[128,4096]{1,0:T(8,128)} fusion(bf16[128,3072]{1,0:T(8,128)(2,1)S(1)} %all_gather.43, bf16[1,3072,4096]{2,1,0:T(8,128)(2,1)} %param.17), kind=kOutput, calls=%fused_computation.50 | convolution fusion | flops 3221225472 | bytes 28049408 | tf_op jit(solution)/shard_map/dot_general | solution.py:78
  135.4 20.6 %fusion.140 = bf16[128,3072]{1,0:T(8,128)(2,1)} fusion(bf16[1,4096,3072]{2,1,0:T(8,128)(2,1)} %param.19, bf16[128,3072]{1,0:T(8,128)(2,1)S(1)} %all_gather.43, bf16[1,3072,4096]{2,1,0:T(8,128)(2,1)} %param.18, f32[128,4096]{1,0:T(8,128)} %fusion.47), kind=kOutput, calls=%fused_computation.87 | convolution fusion | flops 6445989888 | bytes 54001664 | tf_op jit(solution)/shard_map/dot_general | solution.py:141
  170.5 9.7 %collective-permute-done = bf16[64,3072]{1,0:T(8,128)(2,1)S(1)} collective-permute-done((bf16[64,3072]{1,0:T(8,128)(2,1)S(1)}, bf16[64,3072]{1,0:T(8,128)(2,1)S(1)}, u32[]{:S(2)}, u32[]{:S(2)}) %collective-permute-start) | collective-permute-done | bytes 393248 | tf_op jit(solution)/shard_map/ppermute | solution.py:19
  210.4 12.9 %fusion.45 = f32[128,4096]{1,0:T(8,128)} fusion(bf16[128,3072]{1,0:T(8,128)(2,1)S(1)} %all_gather.45, bf16[1,3072,4096]{2,1,0:T(8,128)(2,1)} %param.17), kind=kOutput, calls=%fused_computation.48 | convolution fusion | flops 3221225472 | bytes 28049408 | tf_op jit(solution)/shard_map/dot_general | solution.py:78
  223.4 20.6 %fusion.145 = bf16[128,3072]{1,0:T(8,128)(2,1)} fusion(bf16[1,4096,3072]{2,1,0:T(8,128)(2,1)} %param.19, bf16[128,3072]{1,0:T(8,128)(2,1)S(1)} %all_gather.45, bf16[1,3072,4096]{2,1,0:T(8,128)(2,1)} %param.18, f32[128,4096]{1,0:T(8,128)} %fusion.45), kind=kOutput, calls=%fused_computation.88 | convolution fusion | flops 6445989888 | bytes 54001664 | tf_op jit(solution)/shard_map/dot_general | solution.py:141
  258.5 9.7 %collective-permute-done.1 = bf16[64,3072]{1,0:T(8,128)(2,1)S(1)} collective-permute-done((bf16[64,3072]{1,0:T(8,128)(2,1)S(1)}, bf16[64,3072]{1,0:T(8,128)(2,1)S(1)}, u32[]{:S(2)}, u32[]{:S(2)}) %collective-permute-start.1) | collective-permute-done | bytes 393248 | tf_op jit(solution)/shard_map/ppermute | solution.py:19
  283.8 9.5 %reduce-scatter.23.cloned.1.call-done = bf16[64,3072]{1,0:T(8,128)(2,1)} async-done(((bf16[128,3072]{1,0:T(8,128)(2,1)}), bf16[64,3072]{1,0:T(8,128)(2,1)}) %reduce-scatter.23.cloned.1.call-update) | async-done | bytes 393232 | tf_op jit(solution)/shard_map/reduce_scatter | solution.py:128
  298.4 12.9 %fusion.43 = f32[128,4096]{1,0:T(8,128)} fusion(bf16[128,3072]{1,0:T(8,128)(2,1)S(1)} %all_gather.47, bf16[1,3072,4096]{2,1,0:T(8,128)(2,1)} %param.17), kind=kOutput, calls=%fused_computation.46 | convolution fusion | flops 3221225472 | bytes 28049408 | tf_op jit(solution)/shard_map/dot_general | solution.py:78
  311.3 20.6 %fusion.150 = bf16[128,3072]{1,0:T(8,128)(2,1)} fusion(bf16[1,4096,3072]{2,1,0:T(8,128)(2,1)} %param.19, bf16[128,3072]{1,0:T(8,128)(2,1)S(1)} %all_gather.47, bf16[1,3072,4096]{2,1,0:T(8,128)(2,1)} %param.18, f32[128,4096]{1,0:T(8,128)} %fusion.43), kind=kOutput, calls=%fused_computation.89 | convolution fusion | flops 6445989888 | bytes 54001664 | tf_op jit(solution)/shard_map/dot_general | solution.py:141
  346.4 9.7 %collective-permute-done.2 = bf16[64,3072]{1,0:T(8,128)(2,1)S(1)} collective-permute-done((bf16[64,3072]{1,0:T(8,128)(2,1)S(1)}, bf16[64,3072]{1,0:T(8,128)(2,1)S(1)}, u32[]{:S(2)}, u32[]{:S(2)}) %collective-permute-start.2) | collective-permute-done | bytes 393248 | tf_op jit(solution)/shard_map/ppermute | solution.py:19
  371.8 9.5 %reduce-scatter.27.cloned.1.call-done = bf16[64,3072]{1,0:T(8,128)(2,1)} async-done(((bf16[128,3072]{1,0:T(8,128)(2,1)}), bf16[64,3072]{1,0:T(8,128)(2,1)}) %reduce-scatter.27.cloned.1.call-update) | async-done | bytes 393232 | tf_op jit(solution)/shard_map/reduce_scatter | solution.py:128
  386.5 12.9 %fusion.41 = f32[128,4096]{1,0:T(8,128)} fusion(bf16[128,3072]{1,0:T(8,128)(2,1)S(1)} %all_gather.49, bf16[1,3072,4096]{2,1,0:T(8,128)(2,1)} %param.17), kind=kOutput, calls=%fused_computation.44 | convolution fusion | flops 3221225472 | bytes 28049408 | tf_op jit(solution)/shard_map/dot_general | solution.py:78
  399.5 20.6 %fusion.155 = bf16[128,3072]{1,0:T(8,128)(2,1)} fusion(bf16[1,4096,3072]{2,1,0:T(8,128)(2,1)} %param.19, bf16[128,3072]{1,0:T(8,128)(2,1)S(1)} %all_gather.49, bf16[1,3072,4096]{2,1,0:T(8,128)(2,1)} %param.18, f32[128,4096]{1,0:T(8,128)} %fusion.41), kind=kOutput, calls=%fused_computation.90 | convolution fusion | flops 6445989888 | bytes 54001664 | tf_op jit(solution)/shard_map/dot_general | solution.py:141
  434.5 9.8 %collective-permute-done.3 = bf16[64,3072]{1,0:T(8,128)(2,1)S(1)} collective-permute-done((bf16[64,3072]{1,0:T(8,128)(2,1)S(1)}, bf16[64,3072]{1,0:T(8,128)(2,1)S(1)}, u32[]{:S(2)}, u32[]{:S(2)}) %collective-permute-start.3) | collective-permute-done | bytes 393248 | tf_op jit(solution)/shard_map/ppermute | solution.py:19
  474.6 12.9 %fusion.39 = f32[128,4096]{1,0:T(8,128)} fusion(bf16[128,3072]{1,0:T(8,128)(2,1)S(1)} %all_gather.51, bf16[1,3072,4096]{2,1,0:T(8,128)(2,1)} %param.17), kind=kOutput, calls=%fused_computation.42 | convolution fusion | flops 3221225472 | bytes 28049408 | tf_op jit(solution)/shard_map/dot_general | solution.py:78
  487.6 20.6 %fusion.160 = bf16[128,3072]{1,0:T(8,128)(2,1)} fusion(bf16[1,4096,3072]{2,1,0:T(8,128)(2,1)} %param.19, bf16[128,3072]{1,0:T(8,128)(2,1)S(1)} %all_gather.51, bf16[1,3072,4096]{2,1,0:T(8,128)(2,1)} %param.18, f32[128,4096]{1,0:T(8,128)} %fusion.39), kind=kOutput, calls=%fused_computation.91 | convolution fusion | flops 6445989888 | bytes 54001664 | tf_op jit(solution)/shard_map/dot_general | solution.py:141
  522.4 9.7 %collective-permute-done.4 = bf16[64,3072]{1,0:T(8,128)(2,1)S(1)} collective-permute-done((bf16[64,3072]{1,0:T(8,128)(2,1)S(1)}, bf16[64,3072]{1,0:T(8,128)(2,1)S(1)}, u32[]{:S(2)}, u32[]{:S(2)}) %collective-permute-start.4) | collective-permute-done | bytes 393248 | tf_op jit(solution)/shard_map/ppermute | solution.py:19
  564.9 12.9 %fusion.37 = f32[128,4096]{1,0:T(8,128)} fusion(bf16[128,3072]{1,0:T(8,128)(2,1)S(1)} %all_gather.53, bf16[1,3072,4096]{2,1,0:T(8,128)(2,1)} %param.17), kind=kOutput, calls=%fused_computation.40 | convolution fusion | flops 3221225472 | bytes 28049408 | tf_op jit(solution)/shard_map/dot_general | solution.py:78
  577.8 20.6 %fusion.165 = bf16[128,3072]{1,0:T(8,128)(2,1)} fusion(bf16[1,4096,3072]{2,1,0:T(8,128)(2,1)} %param.19, bf16[128,3072]{1,0:T(8,128)(2,1)S(1)} %all_gather.53, bf16[1,3072,4096]{2,1,0:T(8,128)(2,1)} %param.18, f32[128,4096]{1,0:T(8,128)} %fusion.37), kind=kOutput, calls=%fused_computation.92 | convolution fusion | flops 6445989888 | bytes 54001664 | tf_op jit(solution)/shard_map/dot_general | solution.py:141
  612.6 9.7 %collective-permute-done.5 = bf16[64,3072]{1,0:T(8,128)(2,1)S(1)} collective-permute-done((bf16[64,3072]{1,0:T(8,128)(2,1)S(1)}, bf16[64,3072]{1,0:T(8,128)(2,1)S(1)}, u32[]{:S(2)}, u32[]{:S(2)}) %collective-permute-start.5) | collective-permute-done | bytes 393248 | tf_op jit(solution)/shard_map/ppermute | solution.py:19
  655.2 12.9 %fusion.35 = f32[128,4096]{1,0:T(8,128)} fusion(bf16[128,3072]{1,0:T(8,128)(2,1)S(1)} %all_gather.55, bf16[1,3072,4096]{2,1,0:T(8,128)(2,1)} %param.17), kind=kOutput, calls=%fused_computation.38 | convolution fusion | flops 3221225472 | bytes 28049408 | tf_op jit(solution)/shard_map/dot_general | solution.py:78
  668.2 20.6 %fusion.170 = bf16[128,3072]{1,0:T(8,128)(2,1)} fusion(bf16[1,4096,3072]{2,1,0:T(8,128)(2,1)} %param.19, bf16[128,3072]{1,0:T(8,128)(2,1)S(1)} %all_gather.55, bf16[1,3072,4096]{2,1,0:T(8,128)(2,1)} %param.18, f32[128,4096]{1,0:T(8,128)} %fusion.35), kind=kOutput, calls=%fused_computation.93 | convolution fusion | flops 6445989888 | bytes 54001664 | tf_op jit(solution)/shard_map/dot_general | solution.py:141
  700.9 69.3 %all-reduce.2.cloned.1.call-done = bf16[4,64,3072]{2,1,0:T(8,128)(2,1)} async-done(((bf16[4,64,3072]{2,1,0:T(8,128)(2,1)}), bf16[4,64,3072]{2,1,0:T(8,128)(2,1)}) %all-reduce.2.cloned.1.call-update) | async-done | bytes 1572880 | tf_op jit(solution)/shard_map/psum | solution.py:24
  (333 shorter events, 348.9 us)
Async XLA Ops:
  10.9 31.4 %all-to-all-start = ((s32[4,1,128]{2,1,0:T(1,128)}), s32[4,1,128]{2,1,0:T(1,128)S(1)}, u32[]{:S(2)}, u32[]{:S(2)}) async-start(s32[4,1,128]{2,1,0:T(1,128)} %bitcast.3), calls=%async_computation | async-start | bytes 4096 | tf_op jit(solution)/shard_map/all_to_all | solution.py:194
  42.3 50.2 %copy-start.12 = (f32[1,3072]{1,0:T(1,128)S(1)}, f32[1,3072]{1,0:T(1,128)}, u32[]{:S(2)}) copy-start(f32[1,3072]{1,0:T(1,128)} %param.20) | copy-start | bytes 36868
  42.3 39.9 %all-to-all-start.1 = ((bf16[4,128,3072]{2,1,0:T(8,128)(2,1)}), bf16[4,128,3072]{2,1,0:T(8,128)(2,1)S(1)}, u32[]{:S(2)}, u32[]{:S(2)}) async-start(bf16[4,128,3072]{2,1,0:T(8,128)(2,1)} %bitcast.6), calls=%async_computation.1 | async-start | bytes 6291456 | tf_op jit(solution)/shard_map/all_to_all | solution.py:187
  46.6 70.8 %reduce-scatter.15.cloned.1.call-start = ((), (), s32[]{:S(2)}) async-start(), calls=%async_computation.16 | async-start | bytes 1179648 | tf_op jit(solution)/shard_map/reduce_scatter | solution.py:128
  108.7 56.9 %reduce-scatter.17.cloned.1.call-start = ((), (), s32[]{:S(2)}) async-start(), calls=%async_computation.17 | async-start | bytes 1179648 | tf_op jit(solution)/shard_map/reduce_scatter | solution.py:140
  156.0 49.1 %reduce-scatter.19.cloned.1.call-start = ((), (), s32[]{:S(2)}) async-start(), calls=%async_computation.18 | async-start | bytes 1179648 | tf_op jit(solution)/shard_map/reduce_scatter | solution.py:128
  166.9 13.4 %collective-permute-start = (bf16[64,3072]{1,0:T(8,128)(2,1)S(1)}, bf16[64,3072]{1,0:T(8,128)(2,1)S(1)}, u32[]{:S(2)}, u32[]{:S(2)}) collective-permute-start(bf16[64,3072]{1,0:T(8,128)(2,1)S(1)} %add_convert_fusion.6), channel_id=1, source_target_pairs={{0,2},{2,4},{4,6},{1,3},{3,5},{5,7},{8,10},{10,12},{12,14},{9,11},... | collective-permute-start | bytes 1179656 | tf_op jit(solution)/shard_map/ppermute | solution.py:19
  195.6 57.9 %reduce-scatter.21.cloned.1.call-start = ((), (), s32[]{:S(2)}) async-start(), calls=%async_computation.19 | async-start | bytes 1179648 | tf_op jit(solution)/shard_map/reduce_scatter | solution.py:140
  244.0 49.3 %reduce-scatter.23.cloned.1.call-start = ((), (), s32[]{:S(2)}) async-start(), calls=%async_computation.20 | async-start | bytes 1179648 | tf_op jit(solution)/shard_map/reduce_scatter | solution.py:128
  254.9 13.3 %collective-permute-start.1 = (bf16[64,3072]{1,0:T(8,128)(2,1)S(1)}, bf16[64,3072]{1,0:T(8,128)(2,1)S(1)}, u32[]{:S(2)}, u32[]{:S(2)}) collective-permute-start(bf16[64,3072]{1,0:T(8,128)(2,1)S(1)} %add_convert_fusion.5), channel_id=1, source_target_pairs={{0,2},{2,4},{4,6},{1,3},{3,5},{5,7},{8,10},{10,12},{12,14},{9,11},... | collective-permute-start | bytes 1179656 | tf_op jit(solution)/shard_map/ppermute | solution.py:19
  283.7 57.8 %reduce-scatter.25.cloned.1.call-start = ((), (), s32[]{:S(2)}) async-start(), calls=%async_computation.21 | async-start | bytes 1179648 | tf_op jit(solution)/shard_map/reduce_scatter | solution.py:140
  331.9 49.5 %reduce-scatter.27.cloned.1.call-start = ((), (), s32[]{:S(2)}) async-start(), calls=%async_computation.22 | async-start | bytes 1179648 | tf_op jit(solution)/shard_map/reduce_scatter | solution.py:128
  342.8 13.4 %collective-permute-start.2 = (bf16[64,3072]{1,0:T(8,128)(2,1)S(1)}, bf16[64,3072]{1,0:T(8,128)(2,1)S(1)}, u32[]{:S(2)}, u32[]{:S(2)}) collective-permute-start(bf16[64,3072]{1,0:T(8,128)(2,1)S(1)} %add_convert_fusion.4), channel_id=1, source_target_pairs={{0,2},{2,4},{4,6},{1,3},{3,5},{5,7},{8,10},{10,12},{12,14},{9,11},... | collective-permute-start | bytes 1179656 | tf_op jit(solution)/shard_map/ppermute | solution.py:19
  371.8 57.9 %reduce-scatter.29.cloned.1.call-start = ((), (), s32[]{:S(2)}) async-start(), calls=%async_computation.23 | async-start | bytes 1179648 | tf_op jit(solution)/shard_map/reduce_scatter | solution.py:140
  420.1 49.6 %reduce-scatter.31.cloned.1.call-start = ((), (), s32[]{:S(2)}) async-start(), calls=%async_computation.24 | async-start | bytes 1179648 | tf_op jit(solution)/shard_map/reduce_scatter | solution.py:128
  431.0 13.2 %collective-permute-start.3 = (bf16[64,3072]{1,0:T(8,128)(2,1)S(1)}, bf16[64,3072]{1,0:T(8,128)(2,1)S(1)}, u32[]{:S(2)}, u32[]{:S(2)}) collective-permute-start(bf16[64,3072]{1,0:T(8,128)(2,1)S(1)} %add_convert_fusion.3), channel_id=1, source_target_pairs={{0,2},{2,4},{4,6},{1,3},{3,5},{5,7},{8,10},{10,12},{12,14},{9,11},... | collective-permute-start | bytes 1179656 | tf_op jit(solution)/shard_map/ppermute | solution.py:19
  460.1 57.6 %reduce-scatter.33.cloned.1.call-start = ((), (), s32[]{:S(2)}) async-start(), calls=%async_computation.25 | async-start | bytes 1179648 | tf_op jit(solution)/shard_map/reduce_scatter | solution.py:140
  508.2 51.6 %reduce-scatter.35.cloned.1.call-start = ((), (), s32[]{:S(2)}) async-start(), calls=%async_computation.26 | async-start | bytes 1179648 | tf_op jit(solution)/shard_map/reduce_scatter | solution.py:128
  518.9 13.2 %collective-permute-start.4 = (bf16[64,3072]{1,0:T(8,128)(2,1)S(1)}, bf16[64,3072]{1,0:T(8,128)(2,1)S(1)}, u32[]{:S(2)}, u32[]{:S(2)}) collective-permute-start(bf16[64,3072]{1,0:T(8,128)(2,1)S(1)} %add_convert_fusion.2), channel_id=1, source_target_pairs={{0,2},{2,4},{4,6},{1,3},{3,5},{5,7},{8,10},{10,12},{12,14},{9,11},... | collective-permute-start | bytes 1179656 | tf_op jit(solution)/shard_map/ppermute | solution.py:19
  550.3 57.7 %reduce-scatter.37.cloned.1.call-start = ((), (), s32[]{:S(2)}) async-start(), calls=%async_computation.27 | async-start | bytes 1179648 | tf_op jit(solution)/shard_map/reduce_scatter | solution.py:140
  598.4 51.7 %reduce-scatter.39.cloned.1.call-start = ((), (), s32[]{:S(2)}) async-start(), calls=%async_computation.28 | async-start | bytes 1179648 | tf_op jit(solution)/shard_map/reduce_scatter | solution.py:128
  609.1 13.2 %collective-permute-start.5 = (bf16[64,3072]{1,0:T(8,128)(2,1)S(1)}, bf16[64,3072]{1,0:T(8,128)(2,1)S(1)}, u32[]{:S(2)}, u32[]{:S(2)}) collective-permute-start(bf16[64,3072]{1,0:T(8,128)(2,1)S(1)} %add_convert_fusion.1), channel_id=1, source_target_pairs={{0,2},{2,4},{4,6},{1,3},{3,5},{5,7},{8,10},{10,12},{12,14},{9,11},... | collective-permute-start | bytes 1179656 | tf_op jit(solution)/shard_map/ppermute | solution.py:19
  640.6 57.8 %reduce-scatter.41.cloned.1.call-start = ((), (), s32[]{:S(2)}) async-start(), calls=%async_computation.29 | async-start | bytes 1179648 | tf_op jit(solution)/shard_map/reduce_scatter | solution.py:140
  688.8 81.4 %all-reduce.2.cloned.1.call-start = ((), (), s32[]{:S(2)}) async-start(), calls=%async_computation.30 | async-start | bytes 3145728 | tf_op jit(solution)/shard_map/psum | solution.py:24
  (37 other events, 575.5 us)
Sparse Core Ops, SparseCore 0:
  108.8 8.5 reduce-scatter.14
  156.1 9.3 reduce-scatter.16
  195.7 9.3 reduce-scatter.18
  244.1 9.3 reduce-scatter.20
  283.8 9.4 reduce-scatter.22
  332.0 9.3 reduce-scatter.24
  371.9 9.4 reduce-scatter.26
  420.2 9.3 reduce-scatter.28
  460.3 9.3 reduce-scatter.30
  508.3 9.3 reduce-scatter.32
  550.4 9.4 reduce-scatter.34
  598.5 9.3 reduce-scatter.36
  640.7 9.4 reduce-scatter.38
  688.9 9.3 reduce-scatter.40
  701.0 69.1 all-reduce.1
where the time goes:
time: 790 us; the launch traced here: 779 us
  matrix products  325 us (41%)
  waiting for transfers between devices  294 us (37%)
  other arithmetic  42.7 us (5%)
  local copies, waits for them, and re-layouts  36.5 us (5%)
  blocking collectives  36.5 us (5%)
  starting transfers between devices  29.5 us (4%)
  between operations  15.1 us (2%)
    dot_general x7, matrix products, run_layer(): jnp.dot(hidden, down_local, preferred_element_type=jnp.float32)  144 us
    dot_general x7, matrix products, expand(): gate = jnp.dot(rows_in, gate_local, preferred_element_type=jnp.float32)  90.6 us
    psum x1, waiting for transfers between devices, broadcast(): return lax.psum(block, axis)  69.3 us
    reduce_scatter x7, waiting for transfers between devices, run_layer(): lax.psum_scatter(jnp.dot(hidden, down_local, preferred_element_type=jnp.f...  66.6 us
    reduce_scatter x7, waiting for transfers between devices, run_layer(): lax.psum_scatter(jnp.dot(mixed, out_local, preferred_element_type=jnp.flo...  65.8 us
    ppermute x6, waiting for transfers between devices, shifted(): return lax.ppermute(array, axis, pairs)  58.4 us
    all_to_all x1, waiting for transfers between devices, shards(): lax.all_to_all(send_rows.reshape(group_count, capacity, width), 'dp', spl...  33.7 us
    dot_general x7, matrix products, run_layer(): jnp.dot(mixed, out_local, preferred_element_type=jnp.float32)  32.9 us
  transfers between devices with their start and end apart: 23, of which 22 were waited for; matrix products, arithmetic and copies ran while one was open for 4% of the time, Pallas kernels for 0%

commit v1 on v0

--- a/solution.py
+++ b/solution.py
@@ -1,10 +1,14 @@
 import jax
 import jax.numpy as jnp
 from jax import lax
+from jax.experimental import pallas as pl
+from jax.experimental.pallas import tpu as pltpu
 from jax.sharding import PartitionSpec as P
 
 KV = 8
 HD = 128
+SLOTS = 8
+CHUNK = 256
 
 
 def swapped(value, axis, apart):
@@ -150,6 +154,313 @@
     return shifted(result.astype(jnp.bfloat16), "pipe", 1).astype(result.dtype)
 
 
+def section_kernel(
+    x_ref,
+    cos_ref,
+    sin_ref,
+    bias_ref,
+    gain_one_ref,
+    gain_two_ref,
+    query_ref,
+    pair_ref,
+    out_ref,
+    gate_ref,
+    up_ref,
+    down_ref,
+    result_ref,
+    left_buf,
+    right_buf,
+    tail_buf,
+    full_one,
+    full_two,
+    total,
+    outgoing,
+    incoming,
+    halfway,
+    weight_sem,
+    send_sem,
+    recv_sem,
+):
+    mine = lax.axis_index("tensor")
+    peer = 1 - mine
+    rows = x_ref.shape[0]
+    heads_steps = query_ref.shape[1] // CHUNK
+    hidden_steps = gate_ref.shape[1] // CHUNK
+    my_rows = pl.ds(pl.multiple_of(mine * rows, rows), rows)
+    peer_rows = pl.ds(pl.multiple_of(peer * rows, rows), rows)
+
+    def weight_copies(left, right, tail, index, slot):
+        cols = pl.ds(pl.multiple_of(index * CHUNK, CHUNK), CHUNK)
+        return (
+            pltpu.make_async_copy(left.at[:, cols], left_buf.at[slot], weight_sem.at[0, slot]),
+            pltpu.make_async_copy(right.at[:, cols], right_buf.at[slot], weight_sem.at[1, slot]),
+            pltpu.make_async_copy(tail.at[cols, :], tail_buf.at[slot], weight_sem.at[2, slot]),
+        )
+
+    def attention_copies(index, slot):
+        return weight_copies(query_ref, pair_ref, out_ref, index, slot)
+
+    def hidden_copies(index, slot):
+        return weight_copies(gate_ref, up_ref, down_ref, index, slot)
+
+    for step in range(SLOTS):
+        if step < heads_steps:
+            copies = attention_copies(step, step)
+        else:
+            copies = hidden_copies(step - heads_steps, step)
+        for copy in copies:
+            copy.start()
+
+    barrier = pltpu.get_barrier_semaphore()
+    pl.semaphore_signal(
+        barrier, inc=1, device_id={"tensor": peer}, device_id_type=pl.DeviceIdType.MESH
+    )
+    pl.semaphore_wait(barrier, 1)
+
+    def send(source, target, index):
+        return pltpu.make_async_remote_copy(
+            src_ref=source,
+            dst_ref=target,
+            send_sem=send_sem.at[index],
+            recv_sem=recv_sem.at[index],
+            device_id={"tensor": peer},
+            device_id_type=pl.DeviceIdType.MESH,
+        )
+
+    def share(values, gain, full, index):
+        meansq = jnp.mean(values * values, axis=-1, keepdims=True)
+        full[my_rows, :] = (values * lax.rsqrt(meansq + 1e-05) * gain).astype(jnp.bfloat16)
+        copy = send(full.at[my_rows, :], full.at[my_rows, :], index)
+        copy.start()
+        copy.wait()
+
+    def reduce(index):
+        outgoing[index] = total[peer_rows, :].astype(jnp.bfloat16)
+        copy = send(outgoing.at[index], incoming.at[index], 2 + index)
+        copy.start()
+        copy.wait()
+        own = total[my_rows, :].astype(jnp.bfloat16).astype(jnp.float32)
+        return own + incoming[index].astype(jnp.float32)
+
+    def rotated(values):
+        return values * cos_ref[...] + pltpu.roll(values, HD // 2, 1) * sin_ref[...]
+
+    share(x_ref[...].astype(jnp.float32), gain_one_ref[...], full_one, 0)
+    total[...] = jnp.zeros_like(total)
+
+    def attention_step(step, carry):
+        slot = lax.rem(step, SLOTS)
+        for copy in attention_copies(step, slot):
+            copy.wait()
+        normed = full_one[...]
+        queries = jnp.dot(normed, left_buf[slot], preferred_element_type=jnp.float32)
+        pair = jnp.dot(normed, right_buf[slot], preferred_element_type=jnp.float32)
+        keys = rotated(pair[:, :HD]).astype(jnp.bfloat16)
+        values = pair[:, HD:].astype(jnp.bfloat16)
+        mixed = []
+        for head in range(2):
+            query = rotated(queries[:, head * HD : (head + 1) * HD]).astype(jnp.bfloat16)
+            scores = lax.dot_general(
+                query, keys, (((1,), (1,)), ((), ())), preferred_element_type=jnp.float32
+            )
+            scores = scores * HD ** (-0.5) + bias_ref[...]
+            spread = jnp.exp(scores - jnp.max(scores, axis=-1, keepdims=True))
+            weights = spread / jnp.sum(spread, axis=-1, keepdims=True)
+            mixed.append(
+                jnp.dot(weights.astype(jnp.bfloat16), values, preferred_element_type=jnp.float32)
+            )
+        both = jnp.concatenate(mixed, axis=1).astype(jnp.bfloat16)
+        total[...] += jnp.dot(both, tail_buf[slot], preferred_element_type=jnp.float32)
+        for copy in hidden_copies(step + SLOTS - heads_steps, slot):
+            copy.start()
+        return carry
+
+    lax.fori_loop(0, heads_steps, attention_step, 0)
+
+    halfway[...] = x_ref[...].astype(jnp.float32) + reduce(0)
+    share(halfway[...], gain_two_ref[...], full_two, 1)
+    total[...] = jnp.zeros_like(total)
+
+    def hidden_step(step, carry):
+        slot = lax.rem(step + heads_steps, SLOTS)
+        for copy in hidden_copies(step, slot):
+            copy.wait()
+        normed = full_two[...]
+        gate = jnp.dot(normed, left_buf[slot], preferred_element_type=jnp.float32)
+        upward = jnp.dot(normed, right_buf[slot], preferred_element_type=jnp.float32)
+        hidden = (gate / (1.0 + jnp.exp(-gate)) * upward).astype(jnp.bfloat16)
+        total[...] += jnp.dot(hidden, tail_buf[slot], preferred_element_type=jnp.float32)
+
+        @pl.when(step + SLOTS < hidden_steps)
+        def _():
+            for copy in hidden_copies(step + SLOTS, slot):
+                copy.start()
+
+        return carry
+
+    lax.fori_loop(0, hidden_steps, hidden_step, 0)
+    result_ref[...] = (halfway[...] + reduce(1)).astype(jnp.bfloat16)
+
+
+def run_section(current, cosine, sine, bias, layer_weights):
+    (
+        query_local,
+        pair_local,
+        out_local,
+        gate_local,
+        up_local,
+        down_local,
+        gain_attention,
+        gain_forward,
+    ) = layer_weights
+    rows, width = current.shape
+    resident = pl.BlockSpec(memory_space=pltpu.VMEM)
+    streamed = pl.BlockSpec(memory_space=pl.ANY)
+    return pl.pallas_call(
+        section_kernel,
+        out_shape=jax.ShapeDtypeStruct((rows, width), jnp.bfloat16),
+        in_specs=[resident] * 6 + [streamed] * 6,
+        out_specs=resident,
+        scratch_shapes=[
+            pltpu.VMEM((SLOTS, width, CHUNK), jnp.bfloat16),
+            pltpu.VMEM((SLOTS, width, CHUNK), jnp.bfloat16),
+            pltpu.VMEM((SLOTS, CHUNK, width), jnp.bfloat16),
+            pltpu.VMEM((2 * rows, width), jnp.bfloat16),
+            pltpu.VMEM((2 * rows, width), jnp.bfloat16),
+            pltpu.VMEM((2 * rows, width), jnp.float32),
+            pltpu.VMEM((2, rows, width), jnp.bfloat16),
+            pltpu.VMEM((2, rows, width), jnp.bfloat16),
+            pltpu.VMEM((rows, width), jnp.float32),
+            pltpu.SemaphoreType.DMA((3, SLOTS)),
+            pltpu.SemaphoreType.DMA((4,)),
+            pltpu.SemaphoreType.DMA((4,)),
+        ],
+        compiler_params=pltpu.CompilerParams(
+            collective_id=0, has_side_effects=True, vmem_limit_bytes=60 * 2**20
+        ),
+        cost_estimate=pl.CostEstimate(
+            flops=2 * 2 * rows * 5 * CHUNK * width * 12,
+            bytes_accessed=5 * CHUNK * width * 24,
+            transcendentals=0,
+        ),
+    )(
+        current,
+        cosine,
+        sine,
+        bias,
+        gain_attention[None, :],
+        gain_forward[None, :],
+        query_local,
+        pair_local,
+        out_local,
+        gate_local,
+        up_local,
+        down_local,
+    )
+
+
+def regroup(tokens, destination, micro_count, micro_rows):
+    group_count = lax.axis_size("dp")
+    slab_rows = micro_rows // lax.axis_size("tensor")
+    held_rows, width = tokens.shape
+    capacity = held_rows // 2
+    group_span = micro_count * micro_rows
+    everywhere = lax.all_gather(destination, "dp", axis=0)
+    groups = jnp.arange(group_count, dtype=jnp.int32)
+    target = everywhere // group_span
+    within = everywhere % group_span
+    landing = within // micro_rows * slab_rows + within % slab_rows
+    member = (target[:, None, :] == groups[None, :, None]).astype(jnp.int32)
+    before = jnp.sum((jnp.cumsum(member, axis=2) - member) * member, axis=1)
+    slots = jnp.arange(group_count * capacity, dtype=jnp.int32)
+    me = lax.axis_index("dp")
+    own = lax.dynamic_index_in_dim(target * capacity + before, me, 0, keepdims=False)
+    pack = (slots[:, None] == own[None, :]).astype(jnp.bfloat16)
+    send_rows = jnp.dot(pack, tokens, preferred_element_type=jnp.float32).astype(jnp.bfloat16)
+    got_rows = lax.all_to_all(
+        send_rows.reshape(group_count, capacity, width),
+        "dp",
+        split_axis=0,
+        concat_axis=0,
+        tiled=True,
+    )
+    arrives = (groups[:, None] * capacity + before).reshape(-1)
+    lands = jnp.where(target == me, landing, -1).reshape(-1)
+    order = jnp.arange(held_rows, dtype=jnp.int32)
+    unpack = jnp.dot(
+        (order[:, None] == lands[None, :]).astype(jnp.bfloat16),
+        (arrives[:, None] == slots[None, :]).astype(jnp.bfloat16),
+        preferred_element_type=jnp.float32,
+    ).astype(jnp.bfloat16)
+    return jnp.dot(
+        unpack, got_rows.reshape(-1, width), preferred_element_type=jnp.float32
+    ).astype(jnp.bfloat16)
+
+
+def section_tables(doc_ids):
+    group, micro_rows = doc_ids.shape
+    tensor_count = lax.axis_size("tensor")
+
+    def laid(table):
+        by_slab = table.reshape(group, tensor_count, micro_rows // tensor_count)
+        return jnp.swapaxes(by_slab, 0, 1).reshape(-1)
+
+    places = laid(jax.vmap(doc_positions)(doc_ids))
+    order = laid(jnp.broadcast_to(jnp.arange(micro_rows, dtype=jnp.int32), doc_ids.shape))
+    batch = laid(jnp.broadcast_to(jnp.arange(group, dtype=jnp.int32)[:, None], doc_ids.shape))
+    docs = laid(doc_ids)
+    shown = (
+        (docs[:, None] == docs[None, :])
+        & (batch[:, None] == batch[None, :])
+        & (order[None, :] <= order[:, None])
+    )
+    bias = jnp.where(shown, jnp.float32(0), jnp.float32(-1e30))
+    frequency = 500000.0 ** (-(jnp.arange(HD // 2, dtype=jnp.float32) * 2.0 / HD))
+    angles = places[:, None] * frequency[None, :]
+    cosine, sine = jnp.cos(angles), jnp.sin(angles)
+    return (
+        jnp.concatenate([cosine, cosine], axis=1),
+        jnp.concatenate([-sine, sine], axis=1),
+        bias,
+    )
+
+
+def paired_shards(tokens, destination, segments, layer_weights):
+    pipe_count = lax.axis_size("pipe")
+    micro_count, micro_rows = segments.shape
+    slab_rows = micro_rows // lax.axis_size("tensor")
+    width = tokens.shape[1]
+    group = 2
+    group_rows = group * slab_rows
+    rounds = micro_count // group
+    regrouped = regroup(tokens, destination, micro_count, micro_rows)
+    phase_index = lax.axis_index("pipe")
+    tables = [section_tables(segments[r * group : (r + 1) * group]) for r in range(rounds)]
+    carried = None
+    mine = jnp.zeros((slab_rows, width), jnp.bfloat16)
+    for moment in range(rounds + pipe_count - 1):
+        feed = min(moment, rounds - 1)
+        current = regrouped[feed * group_rows : (feed + 1) * group_rows]
+        if carried is not None:
+            current = jnp.where(phase_index == 0, current, carried)
+        round_index = jnp.clip(moment - phase_index, 0, rounds - 1)
+        cosine, sine, bias = (
+            lax.select_n(round_index, *[table[i] for table in tables]) for i in range(3)
+        )
+        result = run_section(current, cosine, sine, bias, layer_weights)
+        done = moment - (pipe_count - 1)
+        if done >= 0:
+            for inner in range(group):
+                piece = result[inner * slab_rows : (inner + 1) * slab_rows]
+                home = done * group + inner
+                if home != pipe_count - 1:
+                    piece = lax.ppermute(piece, "pipe", [(pipe_count - 1, home)])
+                mine = jnp.where(phase_index == home, piece, mine)
+        if moment < rounds + pipe_count - 2:
+            carried = shifted(result, "pipe", 1)
+    return mine.astype(jnp.float32)
+
+
 def shards(
     tokens,
     destination,
@@ -163,6 +474,18 @@
     attention_gain,
     forward_gain,
 ):
+    if lax.axis_size("tensor") == 2:
+        layer_weights = (
+            query_weight[0],
+            key_value_weight[0],
+            out_weight[0],
+            gate_weight[0],
+            up_weight[0],
+            down_weight[0],
+            attention_gain[0],
+            forward_gain[0],
+        )
+        return paired_shards(tokens, destination, segments, layer_weights)
     group_count = lax.axis_size("dp")
     tensor_count = lax.axis_size("tensor")
     pipe_count = lax.axis_size("pipe")

time: 790 us -> 395 us (0.50); the launches traced: 779 us -> 395 us
  matrix products: 325 us -> 6.13 us
  Pallas kernels: 0 us -> 226 us
  waiting for transfers between devices: 294 us -> 111 us
  local copies, waits for them, and re-layouts: 36.5 us -> 4.41 us
  blocking collectives: 36.5 us -> 8.31 us
  other arithmetic: 42.7 us -> 16.8 us
  between operations: 15.1 us -> 0.23 us
    dot_general x49 -> x2, matrix products: 325 us -> 6.13 us  [the longest x1 3.45 us: regroup(): jnp.dot(unpack, got_rows.reshape(-1, width), preferred_element_type=jnp.f...]
    pallas_call x0 -> x5, Pallas kernels: none -> 226 us  [run_section(): pl.pallas_call(section_kernel, out_shape=jax.ShapeDtypeStruct((rows, widt...]
    reduce_scatter x14 -> x0, waiting for transfers between devices: 132 us -> none  [the longest x7 66.6 us: run_layer(): lax.psum_scatter(jnp.dot(hidden, down_local, preferred_element_type=jnp.f...]
    psum x1 -> x0, waiting for transfers between devices: 69.3 us -> none  [broadcast(): return lax.psum(block, axis)]
    all_gather x14 -> x1, blocking collectives: 36.5 us -> 8.31 us  [regroup(): everywhere = lax.all_gather(destination, 'dp', axis=0)]
    dot_general x2 -> x0, local copies, waits for them, and re-layouts: 17.3 us -> none  [the longest x1 8.67 us: run_layer(): jnp.dot(piece, query_local, preferred_element_type=jnp.float32)]
    scatter x3 -> x0, local copies, waits for them, and re-layouts: 15.1 us -> none  [the longest x1 7.43 us: shards(): regrouped = jnp.zeros((held_rows, width), jnp.bfloat16).at[got_places.res...]
    convert_element_type x25 -> x2, other arithmetic: 14.5 us -> 2.09 us  [the longest x1 2.08 us: paired_shards(): return mine.astype(jnp.float32)]
  transfers between devices with their start and end apart: 23 -> 8, of which waited for: 22 -> 6; matrix products, arithmetic and copies ran while one was open for 4% -> 3% of each run, Pallas kernels for 0% -> 11%
where the time goes in v1:
time: 395 us
  Pallas kernels  226 us (57%)
  waiting for transfers between devices  111 us (28%)
  starting transfers between devices  21.9 us (6%)
  other arithmetic  16.8 us (4%)
  blocking collectives  8.31 us (2%)
  matrix products  6.13 us (2%)
  local copies, waits for them, and re-layouts  4.41 us (1%)
    pallas_call x5, Pallas kernels, run_section(): pl.pallas_call(section_kernel, out_shape=jax.ShapeDtypeStruct((rows, widt...  226 us
    ppermute x4, waiting for transfers between devices, shifted(): return lax.ppermute(array, axis, pairs)  69.8 us
    all_to_all x1, waiting for transfers between devices, regroup(): lax.all_to_all(send_rows.reshape(group_count, capacity, width), 'dp', spl...  28.7 us
    ppermute x4, starting transfers between devices, shifted(): return lax.ppermute(array, axis, pairs)  14.4 us
    ppermute x3, waiting for transfers between devices, paired_shards(): piece = lax.ppermute(piece, 'pipe', [(pipe_count - 1, home)])  12.1 us
    all_gather x1, blocking collectives, regroup(): everywhere = lax.all_gather(destination, 'dp', axis=0)  8.31 us
  transfers between devices with their start and end apart: 8, of which 6 were waited for; matrix products, arithmetic and copies ran while one was open for 3% of the time, Pallas kernels for 11%

profile of v1, /device:TPU:16, one launch (start us, length us, event | category | flops | bytes accessed | tf_op | source)
XLA Modules:
  0.0 394.8 jit_solution(6468486214910766705)
XLA Ops:
  0.0 8.3 %all-gather.1 = s32[4,1,256]{2,1,0:T(1,128)S(1)} all-gather(s32[1,1,256]{2,1,0:T(1,128)} %bitcast.98), channel_id=2, replica_groups=mesh['dp'=4,'pipe'=4,'tensor'=2] {'dp'}, dimensions={0}, use_global_device_ids=true | all-gather | bytes 5120 | tf_op jit(solution)/shard_map/all_gather | solution.py:368
  8.4 4.8 %reduce-window.6 = s32[4,4,2,128]{3,2,1,0:T(2,128)S(1)} reduce-window(s32[4,4,2,128]{3,2,1,0:T(2,128)S(1)} %fusion.9, s32[]{:T(128)} %constant.83.clone.1), window={size=1x1x1x128 pad=0_0x0_0x0_0x127_0}, to_apply=%region_0.1 | reduce-window | flops 520192 | bytes 32772 | tf_op jit(solution)/shard_map/reduce-window
  13.7 2.7 convolution_convert_fusion
  16.4 4.8 %all-to-all-start = ((bf16[4,128,3072]{2,1,0:T(8,128)(2,1)}), bf16[4,128,3072]{2,1,0:T(8,128)(2,1)}, u32[]{:S(2)}, u32[]{:S(2)}) async-start(bf16[4,128,3072]{2,1,0:T(8,128)(2,1)} %bitcast.89), calls=%async_computation | async-start | bytes 6291456 | tf_op jit(solution)/shard_map/all_to_all | solution.py:380
  25.8 1.3 select_select_fusion
  27.1 28.7 %all-to-all-done = bf16[4,128,3072]{2,1,0:T(8,128)(2,1)} async-done(((bf16[4,128,3072]{2,1,0:T(8,128)(2,1)}), bf16[4,128,3072]{2,1,0:T(8,128)(2,1)}, u32[]{:S(2)}, u32[]{:S(2)}) %all-to-all-start) | async-done | bytes 3145760 | tf_op jit(solution)/shard_map/all_to_all | solution.py:380
  55.8 3.5 convolution_convert_fusion.1
  60.2 45.3 %shard_map.109 = bf16[128,3072]{1,0:T(8,128)(2,1)} custom-call(bf16[128,3072]{1,0:T(8,128)(2,1)} %slice.66.x_ref, f32[256,128]{1,0:T(8,128)} %get-tuple-element.41.cos_ref, f32[256,128]{1,0:T(8,128)} %get-tuple-element.18.sin_ref, f32[256,256]{1,0:T(8,128)} %get-tuple-element.25.bias_ref, f32[1,3072]{1,0:T(1,128)} %gain_one_ref.9, f32[1,3072]{1,0:T(1,128)} %gain_two_ref.9, ...), custom_call_target="tpu_custom_call" | custom-call | flops 24159191040 | bytes 94371840 | tf_op jit(solution)/shard_map/pallas_call | solution.py:319
  105.5 3.7 collective-permute-start
  110.1 17.3 %collective-permute-done = bf16[128,3072]{1,0:T(8,128)(2,1)S(1)} collective-permute-done((bf16[128,3072]{1,0:T(8,128)(2,1)}, bf16[128,3072]{1,0:T(8,128)(2,1)S(1)}, u32[]{:S(2)}, u32[]{:S(2)}) %collective-permute-start) | collective-permute-done | bytes 786464 | tf_op jit(solution)/shard_map/ppermute | solution.py:23
  128.4 45.3 %shard_map.110 = bf16[128,3072]{1,0:T(8,128)(2,1)} custom-call(bf16[128,3072]{1,0:T(8,128)(2,1)} %broadcast_select_fusion.3.x_ref, f32[256,128]{1,0:T(8,128)} %get-tuple-element.13.cos_ref, f32[256,128]{1,0:T(8,128)} %get-tuple-element.17.sin_ref, f32[256,256]{1,0:T(8,128)} %get-tuple-element.24.bias_ref, f32[1,3072]{1,0:T(1,128)} %gain_one_ref.9, ...), custom_call_target="tpu_custom_call" | custom-call | flops 24159191040 | bytes 94371840 | tf_op jit(solution)/shard_map/pallas_call | solution.py:319
  173.7 3.5 collective-permute-start.1
  177.2 18.4 %collective-permute-done.1 = bf16[128,3072]{1,0:T(8,128)(2,1)S(1)} collective-permute-done((bf16[128,3072]{1,0:T(8,128)(2,1)}, bf16[128,3072]{1,0:T(8,128)(2,1)S(1)}, u32[]{:S(2)}, u32[]{:S(2)}) %collective-permute-start.1) | collective-permute-done | bytes 786464 | tf_op jit(solution)/shard_map/ppermute | solution.py:23
  196.6 45.3 %shard_map.111 = bf16[128,3072]{1,0:T(8,128)(2,1)} custom-call(bf16[128,3072]{1,0:T(8,128)(2,1)} %broadcast_select_fusion.2.x_ref, f32[256,128]{1,0:T(8,128)} %get-tuple-element.14.cos_ref, f32[256,128]{1,0:T(8,128)} %get-tuple-element.16.sin_ref, f32[256,256]{1,0:T(8,128)} %get-tuple-element.23.bias_ref, f32[1,3072]{1,0:T(1,128)} %gain_one_ref.9, ...), custom_call_target="tpu_custom_call" | custom-call | flops 24159191040 | bytes 94371840 | tf_op jit(solution)/shard_map/pallas_call | solution.py:319
  241.8 3.7 collective-permute-start.2
  245.6 18.2 %collective-permute-done.2 = bf16[128,3072]{1,0:T(8,128)(2,1)S(1)} collective-permute-done((bf16[128,3072]{1,0:T(8,128)(2,1)}, bf16[128,3072]{1,0:T(8,128)(2,1)S(1)}, u32[]{:S(2)}, u32[]{:S(2)}) %collective-permute-start.2) | collective-permute-done | bytes 786464 | tf_op jit(solution)/shard_map/ppermute | solution.py:23
  264.7 45.3 %shard_map.112 = bf16[128,3072]{1,0:T(8,128)(2,1)} custom-call(bf16[128,3072]{1,0:T(8,128)(2,1)} %broadcast_select_fusion.1.x_ref, f32[256,128]{1,0:T(8,128)} %get-tuple-element.42.cos_ref, f32[256,128]{1,0:T(8,128)} %get-tuple-element.15.sin_ref, f32[256,256]{1,0:T(8,128)} %get-tuple-element.22.bias_ref, f32[1,3072]{1,0:T(1,128)} %gain_one_ref.9, ...), custom_call_target="tpu_custom_call" | custom-call | flops 24159191040 | bytes 94371840 | tf_op jit(solution)/shard_map/pallas_call | solution.py:319
  310.0 3.5 collective-permute-start.3
  313.5 1.2 fusion.25
  316.1 15.8 %collective-permute-done.3 = bf16[128,3072]{1,0:T(8,128)(2,1)S(1)} collective-permute-done((bf16[128,3072]{1,0:T(8,128)(2,1)}, bf16[128,3072]{1,0:T(8,128)(2,1)S(1)}, u32[]{:S(2)}, u32[]{:S(2)}) %collective-permute-start.3) | collective-permute-done | bytes 786464 | tf_op jit(solution)/shard_map/ppermute | solution.py:23
  332.9 45.4 %shard_map.113 = bf16[128,3072]{1,0:T(8,128)(2,1)} custom-call(bf16[128,3072]{1,0:T(8,128)(2,1)} %broadcast_select_fusion.x_ref, f32[256,128]{1,0:T(8,128)} %get-tuple-element.12.cos_ref, f32[256,128]{1,0:T(8,128)} %get-tuple-element.5.sin_ref, f32[256,256]{1,0:T(8,128)} %get-tuple-element.21.bias_ref, f32[1,3072]{1,0:T(1,128)} %gain_one_ref.9, ...), custom_call_target="tpu_custom_call" | custom-call | flops 24159191040 | bytes 94371840 | tf_op jit(solution)/shard_map/pallas_call | solution.py:319
  379.3 1.3 collective-permute-start.4
  380.6 12.1 %collective-permute-done.4 = bf16[64,3072]{1,0:T(8,128)(2,1)} collective-permute-done((bf16[64,3072]{1,0:T(8,128)(2,1)S(1)}, bf16[64,3072]{1,0:T(8,128)(2,1)}, u32[]{:S(2)}, u32[]{:S(2)}) %collective-permute-start.4) | collective-permute-done | bytes 393248 | tf_op jit(solution)/shard_map/ppermute | solution.py:457
  392.7 2.1 select_convert_fusion
  (59 shorter events, 13.2 us)
Async XLA Ops:
  0.0 13.7 %copy-start = (bf16[256,3072]{1,0:T(8,128)(2,1)S(1)}, bf16[256,3072]{1,0:T(8,128)(2,1)}, u32[]{:S(2)}) copy-start(bf16[256,3072]{1,0:T(8,128)(2,1)} %param.11) | copy-start | bytes 4718596
  16.4 4.9 %copy-start.2 = (s32[4,128]{1,0:T(4,128)S(1)}, s32[4,128]{1,0:T(4,128)}, u32[]{:S(2)}) copy-start(s32[4,128]{1,0:T(4,128)} %param.13) | copy-start | bytes 6148
  16.4 39.5 %all-to-all-start = ((bf16[4,128,3072]{2,1,0:T(8,128)(2,1)}), bf16[4,128,3072]{2,1,0:T(8,128)(2,1)}, u32[]{:S(2)}, u32[]{:S(2)}) async-start(bf16[4,128,3072]{2,1,0:T(8,128)(2,1)} %bitcast.89), calls=%async_computation | async-start | bytes 6291456 | tf_op jit(solution)/shard_map/all_to_all | solution.py:380
  105.5 21.9 %collective-permute-start = (bf16[128,3072]{1,0:T(8,128)(2,1)}, bf16[128,3072]{1,0:T(8,128)(2,1)S(1)}, u32[]{:S(2)}, u32[]{:S(2)}) collective-permute-start(bf16[128,3072]{1,0:T(8,128)(2,1)} %shard_map.109), channel_id=1, source_target_pairs={{0,2},{2,4},{4,6},{1,3},{3,5},{5,7},{8,10},{10,12},{12,14},{9,11},... | collective-permute-start | bytes 2359304 | tf_op jit(solution)/shard_map/ppermute | solution.py:23
  173.7 21.9 %collective-permute-start.1 = (bf16[128,3072]{1,0:T(8,128)(2,1)}, bf16[128,3072]{1,0:T(8,128)(2,1)S(1)}, u32[]{:S(2)}, u32[]{:S(2)}) collective-permute-start(bf16[128,3072]{1,0:T(8,128)(2,1)} %shard_map.110), channel_id=1, source_target_pairs={{0,2},{2,4},{4,6},{1,3},{3,5},{5,7},{8,10},{10,12},{12,14},{9,11},... | collective-permute-start | bytes 2359304 | tf_op jit(solution)/shard_map/ppermute | solution.py:23
  241.8 21.9 %collective-permute-start.2 = (bf16[128,3072]{1,0:T(8,128)(2,1)}, bf16[128,3072]{1,0:T(8,128)(2,1)S(1)}, u32[]{:S(2)}, u32[]{:S(2)}) collective-permute-start(bf16[128,3072]{1,0:T(8,128)(2,1)} %shard_map.111), channel_id=1, source_target_pairs={{0,2},{2,4},{4,6},{1,3},{3,5},{5,7},{8,10},{10,12},{12,14},{9,11},... | collective-permute-start | bytes 2359304 | tf_op jit(solution)/shard_map/ppermute | solution.py:23
  310.0 21.9 %collective-permute-start.3 = (bf16[128,3072]{1,0:T(8,128)(2,1)}, bf16[128,3072]{1,0:T(8,128)(2,1)S(1)}, u32[]{:S(2)}, u32[]{:S(2)}) collective-permute-start(bf16[128,3072]{1,0:T(8,128)(2,1)} %shard_map.112), channel_id=1, source_target_pairs={{0,2},{2,4},{4,6},{1,3},{3,5},{5,7},{8,10},{10,12},{12,14},{9,11},... | collective-permute-start | bytes 2359304 | tf_op jit(solution)/shard_map/ppermute | solution.py:23
  314.7 65.9 %collective-permute-start.5 = (bf16[64,3072]{1,0:T(8,128)(2,1)S(1)}, bf16[64,3072]{1,0:T(8,128)(2,1)S(1)}, u32[]{:S(2)}, u32[]{:S(2)}) collective-permute-start(bf16[64,3072]{1,0:T(8,128)(2,1)S(1)} %get-tuple-element.11), channel_id=1, source_target_pairs={{6,2},{7,3},{14,10},{15,11},{22,18},{23,19},{30,26},{31,27}} | collective-permute-start | bytes 1179656 | tf_op jit(solution)/shard_map/ppermute | solution.py:457
  315.4 65.3 %collective-permute-start.6 = (bf16[64,3072]{1,0:T(8,128)(2,1)S(1)}, bf16[64,3072]{1,0:T(8,128)(2,1)S(1)}, u32[]{:S(2)}, u32[]{:S(2)}) collective-permute-start(bf16[64,3072]{1,0:T(8,128)(2,1)S(1)} %get-tuple-element.10), channel_id=1, source_target_pairs={{6,0},{7,1},{14,8},{15,9},{22,16},{23,17},{30,24},{31,25}} | collective-permute-start | bytes 1179656 | tf_op jit(solution)/shard_map/ppermute | solution.py:457
  332.9 61.9 %copy-start.1 = (bf16[256,3072]{1,0:T(8,128)(2,1)S(1)}, bf16[256,3072]{1,0:T(8,128)(2,1)}, u32[]{:S(2)}) copy-start(bf16[256,3072]{1,0:T(8,128)(2,1)} %param.11) | copy-start | bytes 4718596
  379.3 13.4 %collective-permute-start.4 = (bf16[64,3072]{1,0:T(8,128)(2,1)S(1)}, bf16[64,3072]{1,0:T(8,128)(2,1)}, u32[]{:S(2)}, u32[]{:S(2)}) collective-permute-start(bf16[64,3072]{1,0:T(8,128)(2,1)S(1)} %slice.60), channel_id=1, source_target_pairs={{6,4},{7,5},{14,12},{15,13},{22,20},{23,21},{30,28},{31,29}} | collective-permute-start | bytes 1179656 | tf_op jit(solution)/shard_map/ppermute | solution.py:457
